TPU v7x, 128 devices: a whole 4x4x4 slice. The times are simulated.
128 devices in a mesh: row: 8 (over x_hi, y), col: 8 (over z, x_lo), layer: 2 (over core).
Axes of the slice: x: 4 (x_hi: 2, x_lo: 2; x = x_hi * 2 + x_lo), y: 4, z: 4, core: 2. Of those that a mesh axis runs over, the one named last changes fastest.
Arguments:
- points: float32 [3, 131072], P(None, ('row', 'col', 'layer')), may hold values from 0 to 1
- counts: int32 [131072], P(('row', 'col', 'layer')), may hold values from 0 to 29
- latent: float32 [131072], P(('row', 'col', 'layer')), may hold values from -4 to 4
- probes: float32 [16, 131072], P(None, ('row', 'col', 'layer')), may hold values from -6 to 6
Outputs:
- applied: float32 [16, 131072], P(None, ('row', 'col', 'layer'))
All inputs are finite; a program needn't handle non-finite values.
Results may differ from a plain program's by a relative error of at most 0.0011.
Values may be sent and summed in bfloat16 or wider, within the bound.
A program may use at most 64 MiB of HBM per device.

v0:
```python
import jax
import jax.numpy as jnp
from jax import lax
from jax.sharding import PartitionSpec as P

LENGTH = 0.25
AMP = 0.02
DISP = 4.0


def kernel_block(row_pts, col_pts):
    d2 = (row_pts[0][:, None] - col_pts[0][None, :]) ** 2
    d2 = d2 + (row_pts[1][:, None] - col_pts[1][None, :]) ** 2
    d2 = d2 + (row_pts[2][:, None] - col_pts[2][None, :]) ** 2
    scaled = jnp.sqrt(d2) * (jnp.sqrt(5.0) / LENGTH)
    return (AMP * (1.0 + scaled + scaled * scaled / 3.0) * jnp.exp(-scaled)).astype(jnp.bfloat16)


def local(points, counts, latent, probes):
    local_pts = points.shape[1]
    mean_val = jnp.exp(latent)
    weight = DISP * mean_val * (DISP + counts.astype(jnp.float32)) / (DISP + mean_val) ** 2
    root = jnp.sqrt(weight)
    carried = (root[None, :] * probes).astype(jnp.bfloat16)
    col_vals = lax.all_gather(carried, "row", axis=1, tiled=True)
    width = lax.axis_size("col") * lax.axis_size("layer")
    everything = lax.all_gather(points, ("row", "col", "layer"), axis=1, tiled=True)
    start = lax.axis_index("row") * (width * local_pts)
    row_pts = lax.dynamic_slice_in_dim(everything, start, width * local_pts, 1)
    grid = everything.reshape(3, lax.axis_size("row"), width, local_pts)
    member = lax.axis_index("col") * lax.axis_size("layer") + lax.axis_index("layer")
    col_pts = lax.dynamic_index_in_dim(grid, member, 2, keepdims=False).reshape(
        3, lax.axis_size("row") * local_pts
    )
    tile_rows, tile_cols = (row_pts, col_pts)
    rows_total = tile_rows.shape[1]
    block = min(1024, rows_total)
    blocks = tile_rows.reshape(3, rows_total // block, block).transpose(1, 0, 2)

    def one_block(block_pts):
        kernel = kernel_block(block_pts, tile_cols)
        return lax.dot_general(
            col_vals, kernel, (((1,), (1,)), ((), ())), preferred_element_type=jnp.float32
        )

    parts = lax.map(one_block, blocks)
    partial_rows = parts.transpose(1, 0, 2).reshape(col_vals.shape[0], rows_total)
    summed = lax.psum_scatter(partial_rows, ("col", "layer"), scatter_dimension=1, tiled=True)
    return probes + root[None, :] * summed


def solution(mesh):
    in_specs = (
        P(None, ("row", "col", "layer")),
        P(("row", "col", "layer")),
        P(("row", "col", "layer")),
        P(None, ("row", "col", "layer")),
    )
    out_specs = P(None, ("row", "col", "layer"))
    return jax.shard_map(local, mesh=mesh, in_specs=in_specs, out_specs=out_specs, check_vma=False)
```

profile of v0, /device:TPU:1, one launch (start us, length us, event | category | flops | bytes accessed | tf_op | source)
XLA Modules:
  0.0 722.5 jit_solution(10710162796647098151)
XLA Ops:
  6.5 0.7 all-gather.2.cloned.1.call-update
  7.3 0.0 reduce-scatter.2.cloned.1.call-start
  7.3 0.7 divide_sqrt_fusion
  8.0 0.6 copy-done.1
  8.6 0.8 multiply_convert_fusion.6
  9.5 29.6 %all_gather.7 = bf16[16,8192]{1,0:T(8,128)(2,1)S(1)} all-gather(bf16[16,1024]{1,0:T(8,128)(2,1)S(1)} %multiply_convert_fusion.6), channel_id=1, replica_groups=mesh['row'=8,'col'=8,'layer'=2] {'row'}, dimensions={1}, use_global_device_ids=true | all-gather | bytes 294912 | tf_op jit(solution)/shard_map/all_gather | solution.py:25
  39.1 167.3 %all-gather.2.cloned.1.call-done = f32[3,131072]{1,0:T(4,128)} async-done(((f32[3,1024]{1,0:T(4,128)}), f32[3,131072]{1,0:T(4,128)}) %all-gather.2.cloned.1.call-update) | async-done | bytes 1572880 | tf_op jit(solution)/shard_map/all_gather | solution.py:27
  206.3 2.5 copy.9
  208.8 0.1 constant_dynamic-slice_fusion.3
  209.0 0.1 copy.10
  209.0 1.0 constant_dynamic-slice_fusion.4
  210.0 446.1 %while.10 = (s32[]{:T(128)}, f32[16,16,1024]{2,1,0:T(8,128)S(1)}, f32[16,3,1024]{2,1,0:T(4,128)S(1)}, f32[3,8192]{1,0:T(4,128)S(1)}, bf16[16,8192]{1,0:T(8,128)(2,1)S(1)}, /*index=5*/s32[]{:T(128)}, s32[]{:T(128)}, s32[]{}, s32[]{}) while((s32[]{:T(128)}, f32[16,16,1024]{2,1,0:T(8,128)S(1)}, f32[16,3,1024]{2,1,0:T(4,128)S(1)}, ...), condition=%wide.region_1.2_spmd, body=%wide.region_0.1_spmd.sunk | while | flops 411041792 | bytes 659589 | solution.py:46
  210.1 0.1 fusion.13
  210.2 27.8 %fusion.14 = f32[16,16,1024]{2,1,0:T(8,128)S(1)} fusion(f32[16,16,1024]{2,1,0:T(8,128)S(1)} %get-tuple-element.102, s32[]{:T(128)} %get-tuple-element.101, bf16[16,8192]{1,0:T(8,128)(2,1)S(1)} %get-tuple-element.114, f32[8192]{0:T(1024)S(1)} %bitcast.50, f32[1024]{0:T(1024)S(1)} %bitcast.56, f32[8192]{0:T(1024)S(1)} %bitcast.51, ...), kind=kOutput, calls=%fused_computation.3.clone.1 | convolution fusion | flops 411041792 | bytes 438276 | tf_op jit(solution)/shard_map/while/body/eval_jaxpr/dot_general | solution.py:42
  238.0 0.1 fusion.13
  238.0 27.8 %fusion.14 = f32[16,16,1024]{2,1,0:T(8,128)S(1)} fusion(f32[16,16,1024]{2,1,0:T(8,128)S(1)} %get-tuple-element.102, s32[]{:T(128)} %get-tuple-element.101, bf16[16,8192]{1,0:T(8,128)(2,1)S(1)} %get-tuple-element.114, f32[8192]{0:T(1024)S(1)} %bitcast.50, f32[1024]{0:T(1024)S(1)} %bitcast.56, f32[8192]{0:T(1024)S(1)} %bitcast.51, ...), kind=kOutput, calls=%fused_computation.3.clone.1 | convolution fusion | flops 411041792 | bytes 438276 | tf_op jit(solution)/shard_map/while/body/eval_jaxpr/dot_general | solution.py:42
  265.8 0.1 fusion.13
  265.9 27.8 %fusion.14 = f32[16,16,1024]{2,1,0:T(8,128)S(1)} fusion(f32[16,16,1024]{2,1,0:T(8,128)S(1)} %get-tuple-element.102, s32[]{:T(128)} %get-tuple-element.101, bf16[16,8192]{1,0:T(8,128)(2,1)S(1)} %get-tuple-element.114, f32[8192]{0:T(1024)S(1)} %bitcast.50, f32[1024]{0:T(1024)S(1)} %bitcast.56, f32[8192]{0:T(1024)S(1)} %bitcast.51, ...), kind=kOutput, calls=%fused_computation.3.clone.1 | convolution fusion | flops 411041792 | bytes 438276 | tf_op jit(solution)/shard_map/while/body/eval_jaxpr/dot_general | solution.py:42
  293.7 0.1 fusion.13
  293.8 27.8 %fusion.14 = f32[16,16,1024]{2,1,0:T(8,128)S(1)} fusion(f32[16,16,1024]{2,1,0:T(8,128)S(1)} %get-tuple-element.102, s32[]{:T(128)} %get-tuple-element.101, bf16[16,8192]{1,0:T(8,128)(2,1)S(1)} %get-tuple-element.114, f32[8192]{0:T(1024)S(1)} %bitcast.50, f32[1024]{0:T(1024)S(1)} %bitcast.56, f32[8192]{0:T(1024)S(1)} %bitcast.51, ...), kind=kOutput, calls=%fused_computation.3.clone.1 | convolution fusion | flops 411041792 | bytes 438276 | tf_op jit(solution)/shard_map/while/body/eval_jaxpr/dot_general | solution.py:42
  321.6 0.1 fusion.13
  321.7 27.8 %fusion.14 = f32[16,16,1024]{2,1,0:T(8,128)S(1)} fusion(f32[16,16,1024]{2,1,0:T(8,128)S(1)} %get-tuple-element.102, s32[]{:T(128)} %get-tuple-element.101, bf16[16,8192]{1,0:T(8,128)(2,1)S(1)} %get-tuple-element.114, f32[8192]{0:T(1024)S(1)} %bitcast.50, f32[1024]{0:T(1024)S(1)} %bitcast.56, f32[8192]{0:T(1024)S(1)} %bitcast.51, ...), kind=kOutput, calls=%fused_computation.3.clone.1 | convolution fusion | flops 411041792 | bytes 438276 | tf_op jit(solution)/shard_map/while/body/eval_jaxpr/dot_general | solution.py:42
  349.5 0.1 fusion.13
  349.6 27.8 %fusion.14 = f32[16,16,1024]{2,1,0:T(8,128)S(1)} fusion(f32[16,16,1024]{2,1,0:T(8,128)S(1)} %get-tuple-element.102, s32[]{:T(128)} %get-tuple-element.101, bf16[16,8192]{1,0:T(8,128)(2,1)S(1)} %get-tuple-element.114, f32[8192]{0:T(1024)S(1)} %bitcast.50, f32[1024]{0:T(1024)S(1)} %bitcast.56, f32[8192]{0:T(1024)S(1)} %bitcast.51, ...), kind=kOutput, calls=%fused_computation.3.clone.1 | convolution fusion | flops 411041792 | bytes 438276 | tf_op jit(solution)/shard_map/while/body/eval_jaxpr/dot_general | solution.py:42
  377.4 0.1 fusion.13
  377.4 27.8 %fusion.14 = f32[16,16,1024]{2,1,0:T(8,128)S(1)} fusion(f32[16,16,1024]{2,1,0:T(8,128)S(1)} %get-tuple-element.102, s32[]{:T(128)} %get-tuple-element.101, bf16[16,8192]{1,0:T(8,128)(2,1)S(1)} %get-tuple-element.114, f32[8192]{0:T(1024)S(1)} %bitcast.50, f32[1024]{0:T(1024)S(1)} %bitcast.56, f32[8192]{0:T(1024)S(1)} %bitcast.51, ...), kind=kOutput, calls=%fused_computation.3.clone.1 | convolution fusion | flops 411041792 | bytes 438276 | tf_op jit(solution)/shard_map/while/body/eval_jaxpr/dot_general | solution.py:42
  405.2 0.1 fusion.13
  405.3 27.8 %fusion.14 = f32[16,16,1024]{2,1,0:T(8,128)S(1)} fusion(f32[16,16,1024]{2,1,0:T(8,128)S(1)} %get-tuple-element.102, s32[]{:T(128)} %get-tuple-element.101, bf16[16,8192]{1,0:T(8,128)(2,1)S(1)} %get-tuple-element.114, f32[8192]{0:T(1024)S(1)} %bitcast.50, f32[1024]{0:T(1024)S(1)} %bitcast.56, f32[8192]{0:T(1024)S(1)} %bitcast.51, ...), kind=kOutput, calls=%fused_computation.3.clone.1 | convolution fusion | flops 411041792 | bytes 438276 | tf_op jit(solution)/shard_map/while/body/eval_jaxpr/dot_general | solution.py:42
  433.1 0.1 fusion.13
  433.2 27.8 %fusion.14 = f32[16,16,1024]{2,1,0:T(8,128)S(1)} fusion(f32[16,16,1024]{2,1,0:T(8,128)S(1)} %get-tuple-element.102, s32[]{:T(128)} %get-tuple-element.101, bf16[16,8192]{1,0:T(8,128)(2,1)S(1)} %get-tuple-element.114, f32[8192]{0:T(1024)S(1)} %bitcast.50, f32[1024]{0:T(1024)S(1)} %bitcast.56, f32[8192]{0:T(1024)S(1)} %bitcast.51, ...), kind=kOutput, calls=%fused_computation.3.clone.1 | convolution fusion | flops 411041792 | bytes 438276 | tf_op jit(solution)/shard_map/while/body/eval_jaxpr/dot_general | solution.py:42
  461.0 0.1 fusion.13
  461.1 27.8 %fusion.14 = f32[16,16,1024]{2,1,0:T(8,128)S(1)} fusion(f32[16,16,1024]{2,1,0:T(8,128)S(1)} %get-tuple-element.102, s32[]{:T(128)} %get-tuple-element.101, bf16[16,8192]{1,0:T(8,128)(2,1)S(1)} %get-tuple-element.114, f32[8192]{0:T(1024)S(1)} %bitcast.50, f32[1024]{0:T(1024)S(1)} %bitcast.56, f32[8192]{0:T(1024)S(1)} %bitcast.51, ...), kind=kOutput, calls=%fused_computation.3.clone.1 | convolution fusion | flops 411041792 | bytes 438276 | tf_op jit(solution)/shard_map/while/body/eval_jaxpr/dot_general | solution.py:42
  488.9 0.1 fusion.13
  489.0 27.8 %fusion.14 = f32[16,16,1024]{2,1,0:T(8,128)S(1)} fusion(f32[16,16,1024]{2,1,0:T(8,128)S(1)} %get-tuple-element.102, s32[]{:T(128)} %get-tuple-element.101, bf16[16,8192]{1,0:T(8,128)(2,1)S(1)} %get-tuple-element.114, f32[8192]{0:T(1024)S(1)} %bitcast.50, f32[1024]{0:T(1024)S(1)} %bitcast.56, f32[8192]{0:T(1024)S(1)} %bitcast.51, ...), kind=kOutput, calls=%fused_computation.3.clone.1 | convolution fusion | flops 411041792 | bytes 438276 | tf_op jit(solution)/shard_map/while/body/eval_jaxpr/dot_general | solution.py:42
  516.8 0.1 fusion.13
  516.8 27.8 %fusion.14 = f32[16,16,1024]{2,1,0:T(8,128)S(1)} fusion(f32[16,16,1024]{2,1,0:T(8,128)S(1)} %get-tuple-element.102, s32[]{:T(128)} %get-tuple-element.101, bf16[16,8192]{1,0:T(8,128)(2,1)S(1)} %get-tuple-element.114, f32[8192]{0:T(1024)S(1)} %bitcast.50, f32[1024]{0:T(1024)S(1)} %bitcast.56, f32[8192]{0:T(1024)S(1)} %bitcast.51, ...), kind=kOutput, calls=%fused_computation.3.clone.1 | convolution fusion | flops 411041792 | bytes 438276 | tf_op jit(solution)/shard_map/while/body/eval_jaxpr/dot_general | solution.py:42
  544.6 0.1 fusion.13
  544.7 27.8 %fusion.14 = f32[16,16,1024]{2,1,0:T(8,128)S(1)} fusion(f32[16,16,1024]{2,1,0:T(8,128)S(1)} %get-tuple-element.102, s32[]{:T(128)} %get-tuple-element.101, bf16[16,8192]{1,0:T(8,128)(2,1)S(1)} %get-tuple-element.114, f32[8192]{0:T(1024)S(1)} %bitcast.50, f32[1024]{0:T(1024)S(1)} %bitcast.56, f32[8192]{0:T(1024)S(1)} %bitcast.51, ...), kind=kOutput, calls=%fused_computation.3.clone.1 | convolution fusion | flops 411041792 | bytes 438276 | tf_op jit(solution)/shard_map/while/body/eval_jaxpr/dot_general | solution.py:42
  572.5 0.1 fusion.13
  572.6 27.8 %fusion.14 = f32[16,16,1024]{2,1,0:T(8,128)S(1)} fusion(f32[16,16,1024]{2,1,0:T(8,128)S(1)} %get-tuple-element.102, s32[]{:T(128)} %get-tuple-element.101, bf16[16,8192]{1,0:T(8,128)(2,1)S(1)} %get-tuple-element.114, f32[8192]{0:T(1024)S(1)} %bitcast.50, f32[1024]{0:T(1024)S(1)} %bitcast.56, f32[8192]{0:T(1024)S(1)} %bitcast.51, ...), kind=kOutput, calls=%fused_computation.3.clone.1 | convolution fusion | flops 411041792 | bytes 438276 | tf_op jit(solution)/shard_map/while/body/eval_jaxpr/dot_general | solution.py:42
  600.4 0.1 fusion.13
  600.5 27.8 %fusion.14 = f32[16,16,1024]{2,1,0:T(8,128)S(1)} fusion(f32[16,16,1024]{2,1,0:T(8,128)S(1)} %get-tuple-element.102, s32[]{:T(128)} %get-tuple-element.101, bf16[16,8192]{1,0:T(8,128)(2,1)S(1)} %get-tuple-element.114, f32[8192]{0:T(1024)S(1)} %bitcast.50, f32[1024]{0:T(1024)S(1)} %bitcast.56, f32[8192]{0:T(1024)S(1)} %bitcast.51, ...), kind=kOutput, calls=%fused_computation.3.clone.1 | convolution fusion | flops 411041792 | bytes 438276 | tf_op jit(solution)/shard_map/while/body/eval_jaxpr/dot_general | solution.py:42
  628.3 0.1 fusion.13
  628.4 27.8 %fusion.14 = f32[16,16,1024]{2,1,0:T(8,128)S(1)} fusion(f32[16,16,1024]{2,1,0:T(8,128)S(1)} %get-tuple-element.102, s32[]{:T(128)} %get-tuple-element.101, bf16[16,8192]{1,0:T(8,128)(2,1)S(1)} %get-tuple-element.114, f32[8192]{0:T(1024)S(1)} %bitcast.50, f32[1024]{0:T(1024)S(1)} %bitcast.56, f32[8192]{0:T(1024)S(1)} %bitcast.51, ...), kind=kOutput, calls=%fused_computation.3.clone.1 | convolution fusion | flops 411041792 | bytes 438276 | tf_op jit(solution)/shard_map/while/body/eval_jaxpr/dot_general | solution.py:42
  656.1 1.1 copy.8
  657.2 0.0 reduce-scatter.2.cloned.1.call-update
  657.2 56.9 %reduce-scatter.2.cloned.1.call-done = f32[16,1024]{1,0:T(8,128)} async-done(((f32[16,16384]{1,0:T(8,128)}), f32[16,1024]{1,0:T(8,128)}) %reduce-scatter.2.cloned.1.call-update) | async-done | bytes 65552 | tf_op jit(solution)/shard_map/reduce_scatter | solution.py:48
  714.1 1.5 multiply_add_fusion
  (24 shorter events, 0.3 us)
Async XLA Ops:
  6.5 199.8 %all-gather.2.cloned.1.call-start = ((), (), s32[]{:S(2)}) async-start(), calls=%async_computation.1 | async-start | bytes 2113536 | tf_op jit(solution)/shard_map/all_gather | solution.py:27
  7.3 706.9 %reduce-scatter.2.cloned.1.call-start = ((), (), s32[]{:S(2)}) async-start(), calls=%async_computation.2 | async-start | bytes 1114112 | tf_op jit(solution)/shard_map/reduce_scatter | solution.py:48
  8.0 0.6 copy-start.1
  656.1 58.0 %copy-start = (f32[16,1024]{1,0:T(8,128)S(1)}, f32[16,1024]{1,0:T(8,128)}, u32[]{:S(2)}) copy-start(f32[16,1024]{1,0:T(8,128)} %param.9) | copy-start | bytes 196612
  656.1 58.0 %copy-start.2 = (f32[1024]{0:T(1024)S(1)}, f32[1024]{0:T(1024)}, u32[]{:S(2)}) copy-start(f32[1024]{0:T(1024)} %copy-done.1) | copy-start | bytes 12292
Sparse Core Ops, SparseCore 0:
  9.1 197.2 all-gather.1
  657.4 56.7 reduce-scatter.1
where the time goes:
time: 726 us; the launch traced here: 722 us
  matrix products  444 us (61%)
  waiting for transfers between devices  225 us (31%)
  blocking collectives  29.6 us (4%)
  between operations  13.5 us (2%)
    dot_general x16, matrix products, one_block(): lax.dot_general(col_vals, kernel, (((1,), (1,)), ((), ())), preferred_ele...  444 us
    all_gather x1, waiting for transfers between devices, local(): lax.all_gather(points, ('row', 'col', 'layer'), axis=1, tiled=True)  167 us
    reduce_scatter x1, waiting for transfers between devices, local(): lax.psum_scatter(partial_rows, ('col', 'layer'), scatter_dimension=1, til...  56.9 us
    all_gather x1, blocking collectives, local(): col_vals = lax.all_gather(carried, 'row', axis=1, tiled=True)  29.6 us
  transfers between devices with their start and end apart: 2, of which 2 were waited for; matrix products, arithmetic and copies ran while one was open for 0% of the time, Pallas kernels for 0%

commit v1 on v0

v1 whole, which is shorter than its diff:
```python
import functools
import math

import jax
import jax.numpy as jnp
from jax import lax
from jax.experimental import pallas as pl
from jax.experimental.pallas import tpu as pltpu
from jax.sharding import PartitionSpec as P

LENGTH = 0.25
AMP = 0.02
DISP = 4.0

MESH = pl.DeviceIdType.MESH
SH = 1024
BI, BJ = 512, 256
DEPTH = 8
FEAT = 64

L2E = math.log2(math.e)
COORD = math.sqrt(5.0) / LENGTH * L2E
H = 1.5 * L2E
D = 0.75 * L2E * L2E
B0 = math.log2(AMP / (3.0 * L2E * L2E))
FLOOR = 3e-5


def entries(u):
    s = u * lax.rsqrt(jnp.maximum(u, FLOOR))
    t = s + H
    return ((t * t + D) * jnp.exp2(B0 - s)).astype(jnp.bfloat16)


def pieces(v):
    high = v.astype(jnp.bfloat16).astype(jnp.float32)
    rest = v - high
    mid = rest.astype(jnp.bfloat16).astype(jnp.float32)
    return high, mid, rest - mid


def features(pts):
    a = (pts - 0.5) * COORD
    norm = jnp.sum(a * a, axis=0, keepdims=True)
    h, m, l = pieces(a)
    nh, nm, nl = pieces(norm)
    at = lax.broadcasted_iota(jnp.int32, a.shape, 0)
    ones = jnp.where(at < 3, 1.0, 0.0)
    sq = jnp.where(at == 0, nh, jnp.where(at == 1, nm, jnp.where(at == 2, nl, 0.0)))
    left = jnp.concatenate([h, h, m, m, h, l, sq, ones], axis=0)
    right = jnp.concatenate([-2.0 * h, -2.0 * m, -2.0 * h, -2.0 * m, -2.0 * l, -2.0 * h, ones, sq], axis=0)
    return left, right


def kernel(groups, members, pts, cnt, lat, prb, out, xs, cs, fi, fj, sums, parts, own, *rest):
    us, ks = rest[:DEPTH], rest[DEPTH : 2 * DEPTH]
    xsend, csend, xrecv, crecv, psend, precv = rest[2 * DEPTH :]
    row, col, layer = lax.axis_index("row"), lax.axis_index("col"), lax.axis_index("layer")
    a = row * 2 + lax.rem(col, 2)
    m = lax.div(col, 2) * 2 + layer
    b = lax.rem(a + m + 1, groups)

    def dev(group, member):
        return (lax.div(group, 2), lax.div(member, 2) * 2 + lax.rem(group, 2), lax.rem(member, 2))

    def mate(k):
        return lax.rem(m + k, members)

    def asker(k):
        return dev(lax.rem(a + groups - k - 1, groups), jnp.int32(k))

    def cols(j):
        return pl.ds(pl.multiple_of(j * SH, SH), SH)

    barrier = pltpu.get_barrier_semaphore()
    for k in range(1, members):
        pl.semaphore_signal(barrier, inc=1, device_id=dev(a, mate(k)), device_id_type=MESH)
    for k in range(members):
        pl.semaphore_signal(barrier, inc=1, device_id=asker(k), device_id_type=MESH)
    for k in range(members):
        pl.semaphore_signal(barrier, inc=1, device_id=dev(b, jnp.int32(k)), device_id_type=MESH)

    mean_val = jnp.exp(lat[...])
    weight = DISP * mean_val * (DISP + cnt[...].astype(jnp.float32)) / (DISP + mean_val) ** 2
    root = jnp.sqrt(weight)
    cs[0, :, cols(m)] = (root * prb[...]).astype(jnp.bfloat16)
    xs[0, m] = jnp.full((8, SH), 0.5, jnp.float32)
    xs[0, m, 0:3, :] = pts[...]
    sums[...] = jnp.zeros_like(sums)
    for k in ks:
        k[...] = jnp.zeros_like(k)

    pl.semaphore_wait(barrier, 3 * members - 1)

    sends = []

    def send(src, dst, ssem, rsem, to):
        copy = pltpu.make_async_remote_copy(
            src_ref=src, dst_ref=dst, send_sem=ssem, recv_sem=rsem, device_id=to, device_id_type=MESH
        )
        copy.start()
        sends.append(copy)

    def shard(which, to, n):
        send(xs.at[0, m], xs.at[which, m], xsend.at[n], xrecv.at[which, m], to)
        send(cs.at[0, :, cols(m)], cs.at[which, :, cols(m)], csend.at[n], crecv.at[which, m], to)

    for k in range(members):
        shard(1, asker(k), k)
        if k:
            shard(0, dev(a, mate(k)), members + k - 1)

    def arrived(ref, sem):
        pltpu.make_async_remote_copy(
            src_ref=ref, dst_ref=ref, send_sem=psend.at[0], recv_sem=sem, device_id=dev(a, mate(1)), device_id_type=MESH
        ).wait_recv()

    def build(which, j):
        left, right = features(xs[which, j])
        fi[which, cols(j), :] = left.T.astype(jnp.bfloat16)
        fj[which, :, cols(j)] = right.astype(jnp.bfloat16)

    build(0, m)
    for blk in range(SH // BI):
        for half in range(BI // BJ):
            at = blk * BI + half * BJ
            rows = pl.ds(pl.multiple_of(m * SH + blk * BI, BI), BI)
            at_cols = pl.ds(pl.multiple_of(m * SH + at, BJ), BJ)
            k = entries(jnp.dot(fi[0, rows, :], fj[0, :, at_cols], preferred_element_type=jnp.float32))
            own[:, at : at + BJ] = jnp.dot(cs[0, :, rows], k, preferred_element_type=jnp.float32)

    for k in range(members):
        if k:
            arrived(xs.at[0, mate(k)], xrecv.at[0, mate(k)])
            arrived(cs.at[0, :, cols(mate(k))], crecv.at[0, mate(k)])
            build(0, mate(k))
        arrived(xs.at[1, k], xrecv.at[1, k])
        arrived(cs.at[1, :, cols(k)], crecv.at[1, k])
        build(1, k)

    ni, nj = members * SH // BI, members * SH // BJ
    inside = jnp.logical_and(m == members - 1, a >= members)
    per = 2 * (ni - 1)
    half_count = (ni // 2) * per
    count = jnp.where(inside, 2 * half_count, ni * nj)

    def place(t):
        t = jnp.minimum(jnp.maximum(t, 0), count - 1)
        j0, i0 = lax.div(t, ni), lax.rem(t, ni)
        side = lax.div(t, half_count)
        r = t - side * half_count
        g = lax.div(r, per)
        r = r - g * per
        n1 = 2 * (ni - 1 - g)
        i1 = jnp.where(r < n1, g, ni - 1 - g)
        j1 = 2 * i1 + 2 + jnp.where(r < n1, r, r - n1)
        i, j = jnp.where(inside, i1, i0), jnp.where(inside, j1, j0)
        si, sj = jnp.where(inside, side, 0), jnp.where(inside, side, 1)
        return si, pl.ds(pl.multiple_of(i * BI, BI), BI), sj, pl.ds(pl.multiple_of(j * BJ, BJ), BJ)

    def distance(t, u):
        si, rows, sj, at_cols = place(t)
        u[...] = jnp.dot(fi[si, rows, :], fj[sj, :, at_cols], preferred_element_type=jnp.float32)

    def products(t, k):
        si, rows, sj, at_cols = place(t)
        kv = k[...]
        sums[sj, :, at_cols] += jnp.dot(cs[si, :, rows], kv, preferred_element_type=jnp.float32)
        sums[si, :, rows] += lax.dot_general(
            cs[sj, :, at_cols], kv, (((1,), (1,)), ((), ())), preferred_element_type=jnp.float32
        )

    distance(jnp.int32(0), us[0])

    def step(p, carry):
        t = p * DEPTH
        for n in range(DEPTH):
            distance(t + n + 1, us[(n + 1) % DEPTH])
            products(t + n - 1, ks[(n - 1) % DEPTH])
            ks[n][...] = entries(us[n][...])
        return carry

    lax.fori_loop(0, lax.div(count, DEPTH), step, 0)
    products(count - 1, ks[DEPTH - 1])

    for k in range(members):
        send(sums.at[1, :, cols(k)], parts.at[members + m], psend.at[k], precv.at[members + m], dev(b, jnp.int32(k)))
        if k:
            send(sums.at[0, :, cols(mate(k))], parts.at[m], psend.at[members + k - 1], precv.at[m], dev(a, mate(k)))
    total = own[...] + sums[0, :, cols(m)]
    for k in range(members):
        arrived(parts.at[members + k], precv.at[members + k])
        total = total + parts[members + k]
        if k:
            arrived(parts.at[mate(k)], precv.at[mate(k)])
            total = total + parts[mate(k)]
    out[...] = prb[...] + root * total
    for copy in sends:
        copy.wait_send()


def local(groups, members, points, counts, latent, probes):
    size = members * SH
    vmem = pl.BlockSpec(memory_space=pltpu.VMEM)
    copies = 2 * members - 1
    return pl.pallas_call(
        functools.partial(kernel, groups, members),
        out_shape=jax.ShapeDtypeStruct(probes.shape, jnp.float32),
        in_specs=[vmem] * 4,
        out_specs=vmem,
        scratch_shapes=[
            pltpu.VMEM((2, members, 8, SH), jnp.float32),
            pltpu.VMEM((2, 16, size), jnp.bfloat16),
            pltpu.VMEM((2, size, FEAT), jnp.bfloat16),
            pltpu.VMEM((2, FEAT, size), jnp.bfloat16),
            pltpu.VMEM((2, 16, size), jnp.float32),
            pltpu.VMEM((2 * members, 16, SH), jnp.float32),
            pltpu.VMEM((16, SH), jnp.float32),
            *[pltpu.VMEM((BI, BJ), jnp.float32)] * DEPTH,
            *[pltpu.VMEM((BI, BJ), jnp.bfloat16)] * DEPTH,
            pltpu.SemaphoreType.DMA((copies,)),
            pltpu.SemaphoreType.DMA((copies,)),
            pltpu.SemaphoreType.DMA((2, members)),
            pltpu.SemaphoreType.DMA((2, members)),
            pltpu.SemaphoreType.DMA((copies,)),
            pltpu.SemaphoreType.DMA((2 * members,)),
        ],
        compiler_params=pltpu.CompilerParams(
            collective_id=0, has_side_effects=True, vmem_limit_bytes=48 * 2**20
        ),
        cost_estimate=pl.CostEstimate(flops=10**10, bytes_accessed=10**7, transcendentals=10**8),
    )(points, counts.reshape(1, SH), latent.reshape(1, SH), probes)


def solution(mesh):
    spec = ("row", "col", "layer")
    groups = mesh.shape["row"] * 2
    members = mesh.shape["col"] // 2 * mesh.shape["layer"]
    return jax.shard_map(
        functools.partial(local, groups, members),
        mesh=mesh,
        in_specs=(P(None, spec), P(spec), P(spec), P(None, spec)),
        out_specs=P(None, spec),
        check_vma=False,
    )
```

time: 726 us -> 144 us (0.20)
  matrix products: 444 us -> 0 us
  waiting for transfers between devices: 225 us -> 0 us
  Pallas kernels: 0 us -> 139 us
  blocking collectives: 29.6 us -> 0 us
  between operations: 13.5 us -> 0.01 us
    dot_general x16 -> x0, matrix products: 444 us -> none  [one_block(): lax.dot_general(col_vals, kernel, (((1,), (1,)), ((), ())), preferred_ele...]
    all_gather x1 -> x0, waiting for transfers between devices: 167 us -> none  [local(): lax.all_gather(points, ('row', 'col', 'layer'), axis=1, tiled=True)]
    pallas_call x0 -> x1, Pallas kernels: none -> 139 us  [local(): pl.pallas_call(functools.partial(kernel, groups, members), out_shape=jax....]
    reduce_scatter x1 -> x0, waiting for transfers between devices: 56.9 us -> none  [local(): lax.psum_scatter(partial_rows, ('col', 'layer'), scatter_dimension=1, til...]
    all_gather x1 -> x0, blocking collectives: 29.6 us -> none  [local(): col_vals = lax.all_gather(carried, 'row', axis=1, tiled=True)]
  transfers between devices with their start and end apart: 2 -> 0, of which waited for: 2 -> 0; matrix products, arithmetic and copies ran while one was open for 0% -> 0% of each run, Pallas kernels for 0% -> 0%
where the time goes in v1:
time: 144 us; the launch traced here: 143 us
  Pallas kernels  139 us (97%)
  local copies, waits for them, and re-layouts  3.56 us (2%)
    pallas_call x1, Pallas kernels, local(): pl.pallas_call(functools.partial(kernel, groups, members), out_shape=jax....  139 us
    unnamed x9, local copies, waits for them, and re-layouts  3.56 us

profile of v1, /device:TPU:1, one launch (start us, length us, event | category | flops | bytes accessed | tf_op | source)
XLA Modules:
  0.0 142.6 jit_solution(10426794912457968428)
XLA Ops:
  0.0 0.0 copy-start
  0.0 0.8 copy-done
  0.8 0.0 copy-start.1
  0.8 0.7 copy-done.1
  1.6 0.0 copy-start.2
  1.6 0.7 copy-done.2
  2.2 0.0 copy-start.3
  2.2 0.7 copy-done.3
  2.9 139.1 %shard_map.46 = f32[16,1024]{1,0:T(8,128)S(1)} custom-call(f32[3,1024]{1,0:T(4,128)S(1)} %copy-done.1, s32[1,1024]{1,0:T(1,128)S(1)} %bitcast.2, f32[1,1024]{1,0:T(1,128)S(1)} %bitcast.3, f32[16,1024]{1,0:T(8,128)S(1)} %copy-done), custom_call_target="tpu_custom_call" | custom-call | flops 10000000000 | bytes 10000000 | tf_op jit(solution)/shard_map/pallas_call | solution.py:206
  142.0 0.6 copy.6
Async XLA Ops:
  0.0 0.8 copy-start
  0.8 0.7 copy-start.1
  1.6 0.7 copy-start.2
  2.2 0.7 copy-start.3

commit v2 on v1

v2 whole, which is shorter than its diff:
```python
import functools
import math

import jax
import jax.numpy as jnp
from jax import lax
from jax.experimental import pallas as pl
from jax.experimental.pallas import tpu as pltpu
from jax.sharding import PartitionSpec as P

LENGTH = 0.25
AMP = 0.02
DISP = 4.0

MESH = pl.DeviceIdType.MESH
SH = 1024
BI, BJ = 512, 256
DEPTH = 8
AHEAD = 5
FEAT = 48

L2E = math.log2(math.e)
COORD = math.sqrt(5.0) / LENGTH * L2E
H = 1.5 * L2E
D = 0.75 * L2E * L2E
B0 = math.log2(AMP / (3.0 * L2E * L2E))
FLOOR = 3e-5


def entries(u):
    s = u * lax.rsqrt(jnp.maximum(u, FLOOR))
    t = s + H
    return ((t * t + D) * jnp.exp2(B0 - s)).astype(jnp.bfloat16)


def pieces(v):
    high = v.astype(jnp.bfloat16).astype(jnp.float32)
    rest = v - high
    mid = rest.astype(jnp.bfloat16).astype(jnp.float32)
    return high, mid, rest - mid


def packed(pts):
    a = (pts - 0.5) * COORD
    at = lax.broadcasted_iota(jnp.int32, a.shape, 0)
    h, m, l = (jnp.where(at < 3, v, 0.0) for v in pieces(a))
    return jnp.concatenate([h + jnp.roll(m, 4, axis=0), l], axis=0).astype(jnp.bfloat16)


def features(packs):
    both = packs.astype(jnp.float32)
    hm, low = both[:8], both[8:]
    mh = jnp.roll(hm, 4, axis=0)
    at = lax.broadcasted_iota(jnp.int32, hm.shape, 0)
    a = jnp.where(at < 3, hm + mh + low, 0.0)
    nh, nm, nl = pieces(jnp.sum(a * a, axis=0, keepdims=True))
    ones = jnp.where(at < 3, 1.0, 0.0)
    sq = jnp.where(at == 0, nh, jnp.where(at == 1, nm, jnp.where(at == 2, nl, 0.0)))
    left = jnp.concatenate([hm, hm, hm, low, sq, ones], axis=0)
    right = jnp.concatenate([-2.0 * hm, -2.0 * mh, -2.0 * low, -2.0 * hm, ones, sq], axis=0)
    return left, right


def plan(members):
    half = members // 2
    shells = []
    for k in range(half):
        shells += [(i, k) for i in range(k)] + [(k, j) for j in range(k + 1)]
    top = members - 1
    pairs = shells + [(i, j) for i in range(half) for j in range(half, members)]
    pairs += [(i, j) for j in range(half) for i in range(half, members)]
    pairs += [(top - i, top - j) for i, j in reversed(shells)]
    outside = [(0, i, 1, j) for i, j in pairs]
    inside = []
    for k in range(1, half):
        for side in (1, 0):
            inside += [(side, i, side, k) for i in range(k)]
    for side in (1, 0):
        inside += [(side, i, side, j) for i in range(members) for j in range(max(half, i + 1), members)]
    first = len(outside) - len(inside)
    inside = [None] * first + inside

    def uses(cells, shard):
        return [n for n, cell in enumerate(cells) if cell and shard in (cell[:2], cell[2:])]

    shards = [(1, k) for k in range(members)] + [(0, k) for k in range(1, members)]
    take = {shard: uses(outside, shard)[0] - 1 for shard in shards}
    order = sorted(shards, key=lambda shard: (take[shard], shard))
    for shard in order[1:]:
        assert first == 0 or take[shard] < first or take[shard] < uses(inside, shard)[0]
    send = {shard: 2 * (n - AHEAD) if n >= AHEAD else -1 for n, shard in enumerate(order)}
    give = []
    for cells in (outside, inside):
        steps, at = {}, 0
        for last, shard in sorted((uses(cells, shard)[-1], shard) for shard in shards):
            at = max(last + 1, at + 1)
            steps[shard] = at
        give.append(steps)
    return outside, inside, first, order, take, send, give


def kernel(groups, members, pts_hbm, cnt_hbm, lat_hbm, prb_hbm, out, pts, cnt, lat, prb, xs, fi, fj, sums, parts, own, *rest):
    us, ks = rest[:DEPTH], rest[DEPTH : 2 * DEPTH]
    load, xsend, xrecv, psend, precv = rest[2 * DEPTH :]
    row, col, layer = lax.axis_index("row"), lax.axis_index("col"), lax.axis_index("layer")
    a = row * 2 + lax.rem(col, 2)
    m = lax.div(col, 2) * 2 + layer
    b = lax.rem(a + m + 1, groups)

    def dev(group, member):
        return (lax.div(group, 2), lax.div(member, 2) * 2 + lax.rem(group, 2), lax.rem(member, 2))

    def mate(k):
        return lax.rem(m + k, members)

    def back(k):
        return lax.rem(m + members - k, members)

    def asker(k):
        return dev(lax.rem(a + groups - k - 1, groups), k)

    def cols(j):
        return pl.ds(pl.multiple_of(j * SH, SH), SH)

    pts[...] = jnp.zeros_like(pts)
    loads = [
        pltpu.make_async_copy(src, dst, load.at[n])
        for n, (src, dst) in enumerate([(pts_hbm, pts.at[0:3]), (cnt_hbm, cnt), (lat_hbm, lat), (prb_hbm, prb)])
    ]
    for copy in loads:
        copy.start()
    barrier = pltpu.get_barrier_semaphore()
    for k in range(members):
        pl.semaphore_signal(barrier, inc=1, device_id=dev(b, back(k)), device_id_type=MESH)
    for k in range(1, members):
        pl.semaphore_signal(barrier, inc=1, device_id=dev(a, mate(k)), device_id_type=MESH)

    sums[...] = jnp.zeros_like(sums)
    for k in ks:
        k[...] = jnp.zeros_like(k)
    for copy in loads:
        copy.wait()

    mean_val = jnp.exp(lat[...])
    weight = DISP * mean_val * (DISP + cnt[...].astype(jnp.float32)) / (DISP + mean_val) ** 2
    root = jnp.sqrt(weight)
    xs[0, m, 0:16, :] = (root * prb[...]).astype(jnp.bfloat16)
    xs[0, m, 16:32, :] = packed(pts[...])

    def build(which, j):
        left, right = features(xs[which, j, 16:32, :])
        fi[which, cols(j), :] = left.T.astype(jnp.bfloat16)
        fj[which, :, cols(j)] = right.astype(jnp.bfloat16)

    build(0, m)
    for first in range(0, SH, BI):
        rows = pl.ds(pl.multiple_of(m * SH + first, BI), BI)
        for at in range(first, SH, BJ):
            at_cols = pl.ds(pl.multiple_of(m * SH + at, BJ), BJ)
            k = entries(jnp.dot(fi[0, rows, :], fj[0, :, at_cols], preferred_element_type=jnp.float32))
            term = jnp.dot(xs[0, m, 0:16, first : first + BI], k, preferred_element_type=jnp.float32)
            if first == 0:
                own[:, at : at + BJ] = term
            else:
                own[:, at : at + BJ] += term
            if at >= first + BI:
                own[:, first : first + BI] += lax.dot_general(
                    xs[0, m, 0:16, at : at + BJ], k, (((1,), (1,)), ((), ())), preferred_element_type=jnp.float32
                )

    pl.semaphore_wait(barrier, 2 * members - 1)

    def remote(src, dst, ssem, rsem, to):
        return pltpu.make_async_remote_copy(
            src_ref=src, dst_ref=dst, send_sem=ssem, recv_sem=rsem, device_id=to, device_id_type=MESH
        )

    def ask(k):
        return remote(xs.at[0, m], xs.at[1, m], xsend.at[k], xrecv.at[1, m], asker(mate(k)))

    def share(k):
        return remote(xs.at[0, m], xs.at[0, m], xsend.at[members - 1 + k], xrecv.at[0, m], dev(a, back(k)))

    outside_cells, inside_cells, first_inside, order, take_at, send_at, give_at = plan(members)
    steps = len(outside_cells)

    for which, k in order[:AHEAD]:
        (ask if which else share)(k).start()

    def arrived(ref, sem):
        remote(ref, ref, psend.at[0], sem, dev(a, mate(1))).wait_recv()

    def take(which, j):
        arrived(xs.at[which, j], xrecv.at[which, j])
        build(which, j)

    inside = jnp.logical_and(m == members - 1, a >= members)
    start = jnp.where(inside, first_inside, 0)

    def look(at, table):
        found = jnp.int32(0)
        for n, value in table.items():
            found = jnp.where(at == n, value, found)
        return found

    def code(which, k):
        return which * members + k

    cells = {}
    for kind, listed in enumerate((outside_cells, inside_cells)):
        for n, at in enumerate(listed):
            if at is not None:
                cells[n + kind * steps] = code(*at[:2]) * 2 * members + code(*at[2:])

    def shard_of(value):
        which = lax.div(value, members)
        k = lax.rem(value, members)
        return which, jnp.where(which == 0, mate(k), back(k))

    kind_at = jnp.where(inside, steps, 0)

    def cell(c):
        return look(jnp.minimum(c, steps - 1) + kind_at, cells)

    def place(at, n):
        si, i = shard_of(lax.div(at, 2 * members))
        sj, j = shard_of(lax.rem(at, 2 * members))
        first, second = (n % (SH // BI)) * BI, (n // (SH // BI)) * BJ
        rows = pl.ds(pl.multiple_of(i * SH + first, BI), BI)
        at_cols = pl.ds(pl.multiple_of(j * SH + second, BJ), BJ)
        return si, rows, sj, at_cols, xs.at[si, i, 0:16, first : first + BI], xs.at[sj, j, 0:16, second : second + BJ]

    def distance(at, n, u):
        si, rows, sj, at_cols, _, _ = place(at, n)
        u[...] = jnp.dot(fi[si, rows, :], fj[sj, :, at_cols], preferred_element_type=jnp.float32)

    def products(at, n, k):
        si, rows, sj, at_cols, ci, cj = place(at, n)
        kv = k[...]
        sums[sj, :, at_cols] += jnp.dot(ci[...], kv, preferred_element_type=jnp.float32)
        sums[si, :, rows] += lax.dot_general(
            cj[...], kv, (((1,), (1,)), ((), ())), preferred_element_type=jnp.float32
        )

    def give_row(k):
        j = mate(k)
        return remote(sums.at[0, :, cols(j)], parts.at[m], psend.at[k - 1], precv.at[m], dev(a, j))

    def give_col(k):
        j = back(k)
        return remote(sums.at[1, :, cols(j)], parts.at[members + m], psend.at[members - 1 + k], precv.at[members + m], dev(b, j))

    sending = {send_at[shard]: code(*shard) + 1 for shard in order[AHEAD:]}
    taking = {take_at[shard]: code(*shard) + 1 for shard in order[1:]}
    giving = {}
    for kind, table in enumerate(give_at):
        for shard, n in table.items():
            if n < steps - 1:
                giving[n + 1 + kind * steps] = code(*shard) + 1

    def due(c):
        return look(c, sending), look(c, taking), look(c + kind_at, giving)

    def transfers(send, arrival, give):
        @pl.when(send + arrival + give > 0)
        def _():
            @pl.when(give > members)
            def _():
                give_col(give - 1 - members).start()

            @pl.when(jnp.logical_and(give > 0, give <= members))
            def _():
                give_row(give - 1).start()

            @pl.when(send > members)
            def _():
                ask(send - 1 - members).start()

            @pl.when(jnp.logical_and(send > 0, send <= members))
            def _():
                share(send - 1).start()

            @pl.when(arrival > 0)
            def _():
                take(*shard_of(arrival - 1))

    def early(c, carry):
        transfers(look(c, sending), look(c, taking), jnp.int32(0))
        return carry

    take(1, back(0))
    lax.fori_loop(0, start, early, 0)
    begin = cell(start)
    distance(begin, 0, us[0])

    def step(c, carry):
        last, this, *events = carry
        transfers(*events)
        after = cell(c + 1)
        for n in range(DEPTH):
            if n == DEPTH - 1:
                distance(after, 0, us[0])
            else:
                distance(this, n + 1, us[n + 1])
            if n == 0:
                products(last, DEPTH - 1, ks[DEPTH - 1])
            else:
                products(this, n - 1, ks[n - 1])
            ks[n][...] = entries(us[n][...])

        return (this, after, *due(c + 1))

    last, *_ = lax.fori_loop(start, steps, step, (begin, begin, *due(start)))
    products(last, DEPTH - 1, ks[DEPTH - 1])
    for kind, table in enumerate(give_at):
        for (which, k), n in table.items():
            if n >= steps - 1:

                @pl.when(inside if kind else jnp.logical_not(inside))
                def _(which=which, k=k):
                    (give_col if which else give_row)(k).start()

    total = own[...] + sums[0, :, cols(m)]
    for k in range(members):
        arrived(parts.at[members + k], precv.at[members + k])
        total = total + parts[members + k]
        if k:
            arrived(parts.at[back(k)], precv.at[back(k)])
            total = total + parts[back(k)]
    out[...] = prb[...] + root * total
    for k in range(members):
        ask(k).wait_send()
        give_col(k).wait_send()
        if k:
            share(k).wait_send()
            give_row(k).wait_send()


def local(groups, members, points, counts, latent, probes):
    assert DEPTH == (SH // BI) * (SH // BJ)
    size = members * SH
    copies = 2 * members - 1
    return pl.pallas_call(
        functools.partial(kernel, groups, members),
        out_shape=jax.ShapeDtypeStruct(probes.shape, jnp.float32),
        in_specs=[pl.BlockSpec(memory_space=pl.ANY)] * 4,
        out_specs=pl.BlockSpec(memory_space=pltpu.VMEM),
        scratch_shapes=[
            pltpu.VMEM((8, SH), jnp.float32),
            pltpu.VMEM((1, SH), jnp.int32),
            pltpu.VMEM((1, SH), jnp.float32),
            pltpu.VMEM((16, SH), jnp.float32),
            pltpu.VMEM((2, members, 32, SH), jnp.bfloat16),
            pltpu.VMEM((2, size, FEAT), jnp.bfloat16),
            pltpu.VMEM((2, FEAT, size), jnp.bfloat16),
            pltpu.VMEM((2, 16, size), jnp.float32),
            pltpu.VMEM((2 * members, 16, SH), jnp.float32),
            pltpu.VMEM((16, SH), jnp.float32),
            *[pltpu.VMEM((BI, BJ), jnp.float32)] * DEPTH,
            *[pltpu.VMEM((BI, BJ), jnp.bfloat16)] * DEPTH,
            pltpu.SemaphoreType.DMA((4,)),
            pltpu.SemaphoreType.DMA((copies,)),
            pltpu.SemaphoreType.DMA((2, members)),
            pltpu.SemaphoreType.DMA((copies,)),
            pltpu.SemaphoreType.DMA((2 * members,)),
        ],
        compiler_params=pltpu.CompilerParams(
            collective_id=0, has_side_effects=True, vmem_limit_bytes=48 * 2**20
        ),
        cost_estimate=pl.CostEstimate(flops=10**10, bytes_accessed=10**7, transcendentals=10**8),
    )(points, counts.reshape(1, SH), latent.reshape(1, SH), probes)


def solution(mesh):
    spec = ("row", "col", "layer")
    groups = mesh.shape["row"] * 2
    members = mesh.shape["col"] // 2 * mesh.shape["layer"]
    return jax.shard_map(
        functools.partial(local, groups, members),
        mesh=mesh,
        in_specs=(P(None, spec), P(spec), P(spec), P(None, spec)),
        out_specs=P(None, spec),
        check_vma=False,
    )
```

time: 144 us -> 137 us (0.951)
  Pallas kernels: 139 us -> 133 us
    pallas_call x1, Pallas kernels: 139 us -> 133 us  [local(): pl.pallas_call(functools.partial(kernel, groups, members), out_shape=jax....]
where the time goes in v2:
time: 137 us; the launch traced here: 136 us
  Pallas kernels  133 us (97%)
  local copies, waits for them, and re-layouts  3.56 us (3%)
    pallas_call x1, Pallas kernels, local(): pl.pallas_call(functools.partial(kernel, groups, members), out_shape=jax....  133 us
    unnamed x9, local copies, waits for them, and re-layouts  3.56 us

profile of v2, /device:TPU:1, one launch (start us, length us, event | category | flops | bytes accessed | tf_op | source)
XLA Modules:
  0.0 136.5 jit_solution(7089403649448530806)
XLA Ops:
  0.0 0.0 copy-start
  0.0 0.8 copy-done
  0.8 0.0 copy-start.1
  0.8 0.7 copy-done.1
  1.6 0.0 copy-start.2
  1.6 0.7 copy-done.2
  2.2 0.0 copy-start.3
  2.2 0.7 copy-done.3
  2.9 132.9 %shard_map.46 = f32[16,1024]{1,0:T(8,128)S(1)} custom-call(f32[3,1024]{1,0:T(4,128)S(1)} %copy-done.1, s32[1,1024]{1,0:T(1,128)S(1)} %bitcast.2, f32[1,1024]{1,0:T(1,128)S(1)} %bitcast.3, f32[16,1024]{1,0:T(8,128)S(1)} %copy-done), custom_call_target="tpu_custom_call" | custom-call | flops 10000000000 | bytes 10000000 | tf_op jit(solution)/shard_map/pallas_call | solution.py:343
  135.9 0.6 copy.6
Async XLA Ops:
  0.0 0.8 copy-start
  0.8 0.7 copy-start.1
  1.6 0.7 copy-start.2
  2.2 0.7 copy-start.3

commit v3 on v2

--- a/solution.py
+++ b/solution.py
@@ -15,8 +15,9 @@
 MESH = pl.DeviceIdType.MESH
 SH = 1024
 BI, BJ = 512, 256
-DEPTH = 8
-AHEAD = 5
+TILES = (SH // BI) * (SH // BJ)
+WIDE = 2
+DEPTH = TILES * WIDE
 FEAT = 48
 
 L2E = math.log2(math.e)
@@ -24,11 +25,11 @@
 H = 1.5 * L2E
 D = 0.75 * L2E * L2E
 B0 = math.log2(AMP / (3.0 * L2E * L2E))
-FLOOR = 3e-5
+UP = 2.0**-13
 
 
 def entries(u):
-    s = u * lax.rsqrt(jnp.maximum(u, FLOOR))
+    s = u * lax.rsqrt(u)
     t = s + H
     return ((t * t + D) * jnp.exp2(B0 - s)).astype(jnp.bfloat16)
 
@@ -53,7 +54,7 @@
     mh = jnp.roll(hm, 4, axis=0)
     at = lax.broadcasted_iota(jnp.int32, hm.shape, 0)
     a = jnp.where(at < 3, hm + mh + low, 0.0)
-    nh, nm, nl = pieces(jnp.sum(a * a, axis=0, keepdims=True))
+    nh, nm, nl = pieces(jnp.sum(a * a, axis=0, keepdims=True) + UP)
     ones = jnp.where(at < 3, 1.0, 0.0)
     sq = jnp.where(at == 0, nh, jnp.where(at == 1, nm, jnp.where(at == 2, nl, 0.0)))
     left = jnp.concatenate([hm, hm, hm, low, sq, ones], axis=0)
@@ -63,20 +64,15 @@
 
 def plan(members):
     half = members // 2
-    shells = []
-    for k in range(half):
-        shells += [(i, k) for i in range(k)] + [(k, j) for j in range(k + 1)]
     top = members - 1
-    pairs = shells + [(i, j) for i in range(half) for j in range(half, members)]
-    pairs += [(i, j) for j in range(half) for i in range(half, members)]
-    pairs += [(top - i, top - j) for i, j in reversed(shells)]
+    low, high = range(half), range(half, members)
+    pairs = [(i, j) for j in low for i in low] + [(i, j) for j in low for i in high]
+    pairs += [(i, j) for i in low for j in high]
+    for k in high:
+        pairs += [(k, j) for j in range(top, k - 1, -1)] + [(i, k) for i in range(top, k, -1)]
     outside = [(0, i, 1, j) for i, j in pairs]
-    inside = []
-    for k in range(1, half):
-        for side in (1, 0):
-            inside += [(side, i, side, k) for i in range(k)]
-    for side in (1, 0):
-        inside += [(side, i, side, j) for i in range(members) for j in range(max(half, i + 1), members)]
+    inside = [(side, i, side, j) for side in (0, 1) for j in low for i in range(j)]
+    inside += [(side, i, side, j) for side in (0, 1) for i in range(members) for j in range(max(half, i + 1), members)]
     first = len(outside) - len(inside)
     inside = [None] * first + inside
 
@@ -85,10 +81,10 @@
 
     shards = [(1, k) for k in range(members)] + [(0, k) for k in range(1, members)]
     take = {shard: uses(outside, shard)[0] - 1 for shard in shards}
-    order = sorted(shards, key=lambda shard: (take[shard], shard))
-    for shard in order[1:]:
-        assert first == 0 or take[shard] < first or take[shard] < uses(inside, shard)[0]
-    send = {shard: 2 * (n - AHEAD) if n >= AHEAD else -1 for n, shard in enumerate(order)}
+    for shard in shards:
+        take[shard] = -1 if take[shard] < half - 1 else take[shard]
+        assert take[shard] < first or take[shard] < uses(inside, shard)[0]
+    send = {k: 2 * (k - half) if k >= half else -1 for k in range(1, members)}
     give = []
     for cells in (outside, inside):
         steps, at = {}, 0
@@ -96,7 +92,7 @@
             at = max(last + 1, at + 1)
             steps[shard] = at
         give.append(steps)
-    return outside, inside, first, order, take, send, give
+    return outside, inside, first, take, send, give
 
 
 def kernel(groups, members, pts_hbm, cnt_hbm, lat_hbm, prb_hbm, out, pts, cnt, lat, prb, xs, fi, fj, sums, parts, own, *rest):
@@ -116,8 +112,7 @@
     def back(k):
         return lax.rem(m + members - k, members)
 
-    def asker(k):
-        return dev(lax.rem(a + groups - k - 1, groups), k)
+    asker = dev(lax.rem(a + groups - m - 1, groups), m)
 
     def cols(j):
         return pl.ds(pl.multiple_of(j * SH, SH), SH)
@@ -130,8 +125,7 @@
     for copy in loads:
         copy.start()
     barrier = pltpu.get_barrier_semaphore()
-    for k in range(members):
-        pl.semaphore_signal(barrier, inc=1, device_id=dev(b, back(k)), device_id_type=MESH)
+    pl.semaphore_signal(barrier, inc=1, device_id=dev(b, m), device_id_type=MESH)
     for k in range(1, members):
         pl.semaphore_signal(barrier, inc=1, device_id=dev(a, mate(k)), device_id_type=MESH)
 
@@ -147,12 +141,16 @@
     xs[0, m, 0:16, :] = (root * prb[...]).astype(jnp.bfloat16)
     xs[0, m, 16:32, :] = packed(pts[...])
 
-    def build(which, j):
-        left, right = features(xs[which, j, 16:32, :])
-        fi[which, cols(j), :] = left.T.astype(jnp.bfloat16)
-        fj[which, :, cols(j)] = right.astype(jnp.bfloat16)
-
-    build(0, m)
+    inside = jnp.logical_and(m == members - 1, a >= members)
+
+    def build_left(which, j):
+        fi[which, cols(j), :] = features(xs[which, j, 16:32, :])[0].T.astype(jnp.bfloat16)
+
+    def build_right(which, j):
+        fj[which, :, cols(j)] = features(xs[which, j, 16:32, :])[1].astype(jnp.bfloat16)
+
+    build_left(0, m)
+    build_right(0, m)
     for first in range(0, SH, BI):
         rows = pl.ds(pl.multiple_of(m * SH + first, BI), BI)
         for at in range(first, SH, BJ):
@@ -168,7 +166,7 @@
                     xs[0, m, 0:16, at : at + BJ], k, (((1,), (1,)), ((), ())), preferred_element_type=jnp.float32
                 )
 
-    pl.semaphore_wait(barrier, 2 * members - 1)
+    pl.semaphore_wait(barrier, members)
 
     def remote(src, dst, ssem, rsem, to):
         return pltpu.make_async_remote_copy(
@@ -176,25 +174,42 @@
         )
 
     def ask(k):
-        return remote(xs.at[0, m], xs.at[1, m], xsend.at[k], xrecv.at[1, m], asker(mate(k)))
+        j = mate(k)
+        return remote(xs.at[0, j], xs.at[1, j], xsend.at[k], xrecv.at[1, j], asker)
 
     def share(k):
         return remote(xs.at[0, m], xs.at[0, m], xsend.at[members - 1 + k], xrecv.at[0, m], dev(a, back(k)))
 
-    outside_cells, inside_cells, first_inside, order, take_at, send_at, give_at = plan(members)
+    outside_cells, inside_cells, first_inside, take_at, send_at, give_at = plan(members)
     steps = len(outside_cells)
 
-    for which, k in order[:AHEAD]:
-        (ask if which else share)(k).start()
+    ask(0).start()
+    for k, n in send_at.items():
+        if n < 0:
+            share(k).start()
 
     def arrived(ref, sem):
         remote(ref, ref, psend.at[0], sem, dev(a, mate(1))).wait_recv()
 
-    def take(which, j):
-        arrived(xs.at[which, j], xrecv.at[which, j])
-        build(which, j)
-
-    inside = jnp.logical_and(m == members - 1, a >= members)
+    def take_first(k):
+        j = mate(k)
+        arrived(xs.at[0, j], xrecv.at[0, j])
+        ask(k).start()
+        build_left(0, j)
+
+        @pl.when(inside)
+        def _():
+            build_right(0, j)
+
+    def take_second(k):
+        j = mate(k)
+        arrived(xs.at[1, j], xrecv.at[1, j])
+        build_right(1, j)
+
+        @pl.when(inside)
+        def _():
+            build_left(1, j)
+
     start = jnp.where(inside, first_inside, 0)
 
     def look(at, table):
@@ -215,7 +230,7 @@
     def shard_of(value):
         which = lax.div(value, members)
         k = lax.rem(value, members)
-        return which, jnp.where(which == 0, mate(k), back(k))
+        return which, mate(k)
 
     kind_at = jnp.where(inside, steps, 0)
 
@@ -225,7 +240,7 @@
     def place(at, n):
         si, i = shard_of(lax.div(at, 2 * members))
         sj, j = shard_of(lax.rem(at, 2 * members))
-        first, second = (n % (SH // BI)) * BI, (n // (SH // BI)) * BJ
+        first, second = (n % (SH // BI)) * BI, (n % TILES // (SH // BI)) * BJ
         rows = pl.ds(pl.multiple_of(i * SH + first, BI), BI)
         at_cols = pl.ds(pl.multiple_of(j * SH + second, BJ), BJ)
         return si, rows, sj, at_cols, xs.at[si, i, 0:16, first : first + BI], xs.at[sj, j, 0:16, second : second + BJ]
@@ -247,86 +262,99 @@
         return remote(sums.at[0, :, cols(j)], parts.at[m], psend.at[k - 1], precv.at[m], dev(a, j))
 
     def give_col(k):
-        j = back(k)
+        j = mate(k)
         return remote(sums.at[1, :, cols(j)], parts.at[members + m], psend.at[members - 1 + k], precv.at[members + m], dev(b, j))
 
-    sending = {send_at[shard]: code(*shard) + 1 for shard in order[AHEAD:]}
-    taking = {take_at[shard]: code(*shard) + 1 for shard in order[1:]}
-    giving = {}
+    sending = {n: k for k, n in send_at.items() if n >= 0}
+    taking = {n: code(*shard) + 1 for shard, n in take_at.items() if n >= 0}
+    giving, after_loop = {}, []
     for kind, table in enumerate(give_at):
         for shard, n in table.items():
-            if n < steps - 1:
+            if n + 1 <= steps - WIDE:
                 giving[n + 1 + kind * steps] = code(*shard) + 1
-
-    def due(c):
-        return look(c, sending), look(c, taking), look(c + kind_at, giving)
-
-    def transfers(send, arrival, give):
-        @pl.when(send + arrival + give > 0)
-        def _():
-            @pl.when(give > members)
-            def _():
-                give_col(give - 1 - members).start()
-
-            @pl.when(jnp.logical_and(give > 0, give <= members))
-            def _():
-                give_row(give - 1).start()
-
-            @pl.when(send > members)
-            def _():
-                ask(send - 1 - members).start()
-
-            @pl.when(jnp.logical_and(send > 0, send <= members))
-            def _():
-                share(send - 1).start()
-
-            @pl.when(arrival > 0)
-            def _():
-                take(*shard_of(arrival - 1))
-
-    def early(c, carry):
-        transfers(look(c, sending), look(c, taking), jnp.int32(0))
+            else:
+                after_loop.append((n, kind, shard))
+
+    def fetch_events(c):
+        return [(look(c + n, sending), look(c + n, taking)) for n in range(WIDE)]
+
+    def give_events(c):
+        return [look(c - n + kind_at, giving) for n in range(WIDE)]
+
+    def fetch(events):
+        for send, arrival in events:
+
+            @pl.when(send > 0)
+            def _(send=send):
+                share(send).start()
+
+            @pl.when(arrival > members)
+            def _(arrival=arrival):
+                take_second(arrival - 1 - members)
+
+            @pl.when(jnp.logical_and(arrival > 0, arrival <= members))
+            def _(arrival=arrival):
+                take_first(arrival - 1)
+
+    def give(events):
+        for shard in events:
+
+            @pl.when(shard > members)
+            def _(shard=shard):
+                give_col(shard - 1 - members).start()
+
+            @pl.when(jnp.logical_and(shard > 0, shard <= members))
+            def _(shard=shard):
+                give_row(shard - 1).start()
+
+    for (which, k), n in sorted(take_at.items()):
+        if n < 0 and which == 0:
+            take_first(k)
+    take_second(0)
+
+    def early(p, carry):
+        fetch(fetch_events(p * WIDE))
         return carry
 
-    take(1, back(0))
-    lax.fori_loop(0, start, early, 0)
+    lax.fori_loop(0, lax.div(start, WIDE), early, 0)
     begin = cell(start)
     distance(begin, 0, us[0])
 
-    def step(c, carry):
-        last, this, *events = carry
-        transfers(*events)
-        after = cell(c + 1)
+    def step(p, carry):
+        last, this, events, given = carry
+        any_event = sum(given)
+        for send, arrival in events:
+            any_event = any_event + send + arrival
+
+        @pl.when(any_event > 0)
+        def _():
+            give(given)
+            fetch(events)
+
+        c = p * WIDE
+        held = [this, *[cell(c + n) for n in range(1, WIDE + 1)]]
         for n in range(DEPTH):
-            if n == DEPTH - 1:
-                distance(after, 0, us[0])
-            else:
-                distance(this, n + 1, us[n + 1])
-            if n == 0:
-                products(last, DEPTH - 1, ks[DEPTH - 1])
-            else:
-                products(this, n - 1, ks[n - 1])
+            distance(held[(n + 1) // TILES], n + 1, us[(n + 1) % DEPTH])
+            products(held[(n - 1) // TILES] if n else last, n - 1, ks[(n - 1) % DEPTH])
             ks[n][...] = entries(us[n][...])
-
-        return (this, after, *due(c + 1))
-
-    last, *_ = lax.fori_loop(start, steps, step, (begin, begin, *due(start)))
+        return held[-2], held[-1], fetch_events(c + WIDE), give_events(c + WIDE)
+
+    carry = (begin, begin, fetch_events(start), give_events(start))
+    last, *_ = lax.fori_loop(lax.div(start, WIDE), steps // WIDE, step, carry)
     products(last, DEPTH - 1, ks[DEPTH - 1])
-    for kind, table in enumerate(give_at):
-        for (which, k), n in table.items():
-            if n >= steps - 1:
-
-                @pl.when(inside if kind else jnp.logical_not(inside))
-                def _(which=which, k=k):
-                    (give_col if which else give_row)(k).start()
+    for n, kind, (which, k) in sorted(after_loop):
+
+        @pl.when(inside if kind else jnp.logical_not(inside))
+        def _(which=which, k=k):
+            (give_col if which else give_row)(k).start()
 
     total = own[...] + sums[0, :, cols(m)]
     for k in range(members):
         arrived(parts.at[members + k], precv.at[members + k])
         total = total + parts[members + k]
         if k:
-            arrived(parts.at[back(k)], precv.at[back(k)])
-            total = total + parts[back(k)]
+            arrived(parts.at[mate(k)], precv.at[mate(k)])
+            total = total + parts[mate(k)]
     out[...] = prb[...] + root * total
     for k in range(members):
         ask(k).wait_send()
@@ -337,7 +365,6 @@
 
 
 def local(groups, members, points, counts, latent, probes):
-    assert DEPTH == (SH // BI) * (SH // BJ)
     size = members * SH
     copies = 2 * members - 1
     return pl.pallas_call(
@@ -365,7 +392,7 @@
             pltpu.SemaphoreType.DMA((2 * members,)),
         ],
         compiler_params=pltpu.CompilerParams(
-            collective_id=0, has_side_effects=True, vmem_limit_bytes=48 * 2**20
+            collective_id=0, has_side_effects=True, vmem_limit_bytes=60 * 2**20
         ),
         cost_estimate=pl.CostEstimate(flops=10**10, bytes_accessed=10**7, transcendentals=10**8),
     )(points, counts.reshape(1, SH), latent.reshape(1, SH), probes)

time: 137 us -> 123 us (0.90)
  Pallas kernels: 133 us -> 121 us
  local copies, waits for them, and re-layouts: 3.56 us -> 1.47 us
    pallas_call x1, Pallas kernels: 133 us -> 121 us  [local(): pl.pallas_call(functools.partial(kernel, groups, members), out_shape=jax....]
    unnamed x9 -> x1, local copies, waits for them, and re-layouts: 3.56 us -> 1.47 us
where the time goes in v3:
time: 123 us
  Pallas kernels  121 us (98%)
  local copies, waits for them, and re-layouts  1.47 us (1%)
    pallas_call x1, Pallas kernels, local(): pl.pallas_call(functools.partial(kernel, groups, members), out_shape=jax....  121 us

profile of v3, /device:TPU:1, one launch (start us, length us, event | category | flops | bytes accessed | tf_op | source)
XLA Modules:
  0.0 122.9 jit_solution(1827458798382522706)
XLA Ops:
  0.0 121.4 %shard_map.46 = f32[16,1024]{1,0:T(8,128)} custom-call(f32[3,1024]{1,0:T(4,128)} %pts_hbm.1, s32[1,1024]{1,0:T(1,128)} %bitcast.2, f32[1,1024]{1,0:T(1,128)} %bitcast.3, f32[16,1024]{1,0:T(8,128)} %prb_hbm.1), custom_call_target="tpu_custom_call" | custom-call | flops 10000000000 | bytes 10000000 | tf_op jit(solution)/shard_map/pallas_call | solution.py:370
  121.4 1.5 %copy.6 = f32[16,1024]{1,0:T(8,128)} copy(f32[16,1024]{1,0:T(8,128)} %shard_map.46) | data formatting | bytes 131072

commit v4 on v3

--- a/solution.py
+++ b/solution.py
@@ -14,7 +14,7 @@
 
 MESH = pl.DeviceIdType.MESH
 SH = 1024
-BI, BJ = 512, 256
+BI, BJ = 256, 256
 TILES = (SH // BI) * (SH // BJ)
 WIDE = 2
 DEPTH = TILES * WIDE
@@ -23,15 +23,14 @@
 L2E = math.log2(math.e)
 COORD = math.sqrt(5.0) / LENGTH * L2E
 H = 1.5 * L2E
-D = 0.75 * L2E * L2E
+C = 3.0 * L2E * L2E
 B0 = math.log2(AMP / (3.0 * L2E * L2E))
 UP = 2.0**-13
 
 
-def entries(u):
-    s = u * lax.rsqrt(u)
-    t = s + H
-    return ((t * t + D) * jnp.exp2(B0 - s)).astype(jnp.bfloat16)
+def entries(square, more):
+    s = square * lax.rsqrt(square)
+    return ((more + (2.0 * H) * s) * jnp.exp2(B0 - s)).astype(jnp.bfloat16)
 
 
 def pieces(v):
@@ -54,25 +53,23 @@
     mh = jnp.roll(hm, 4, axis=0)
     at = lax.broadcasted_iota(jnp.int32, hm.shape, 0)
     a = jnp.where(at < 3, hm + mh + low, 0.0)
-    nh, nm, nl = pieces(jnp.sum(a * a, axis=0, keepdims=True) + UP)
+    norm = jnp.sum(a * a, axis=0, keepdims=True) + UP
     ones = jnp.where(at < 3, 1.0, 0.0)
-    sq = jnp.where(at == 0, nh, jnp.where(at == 1, nm, jnp.where(at == 2, nl, 0.0)))
-    left = jnp.concatenate([hm, hm, hm, low, sq, ones], axis=0)
-    right = jnp.concatenate([-2.0 * hm, -2.0 * mh, -2.0 * low, -2.0 * hm, ones, sq], axis=0)
-    return left, right
+
+    def rows(v):
+        high, mid, low = pieces(v)
+        return jnp.where(at == 0, high, jnp.where(at == 1, mid, jnp.where(at == 2, low, 0.0)))
+
+    left = jnp.concatenate([hm, hm, hm, low, rows(norm), ones], axis=0)
+    right = [-2.0 * hm, -2.0 * mh, -2.0 * low, -2.0 * hm, ones]
+    return left, jnp.concatenate([*right, rows(norm), *right, rows(norm + C)], axis=0)
 
 
 def plan(members):
-    half = members // 2
-    top = members - 1
-    low, high = range(half), range(half, members)
-    pairs = [(i, j) for j in low for i in low] + [(i, j) for j in low for i in high]
-    pairs += [(i, j) for i in low for j in high]
-    for k in high:
-        pairs += [(k, j) for j in range(top, k - 1, -1)] + [(i, k) for i in range(top, k, -1)]
+    own_last = [*range(1, members), 0]
+    pairs = [(i, j) for j in range(members) for i in (own_last if j == members - 1 else range(members))]
     outside = [(0, i, 1, j) for i, j in pairs]
-    inside = [(side, i, side, j) for side in (0, 1) for j in low for i in range(j)]
-    inside += [(side, i, side, j) for side in (0, 1) for i in range(members) for j in range(max(half, i + 1), members)]
+    inside = [(side, i, side, j) for side in (0, 1) for j in range(members) for i in range(j)]
     first = len(outside) - len(inside)
     inside = [None] * first + inside
 
@@ -82,9 +79,9 @@
     shards = [(1, k) for k in range(members)] + [(0, k) for k in range(1, members)]
     take = {shard: uses(outside, shard)[0] - 1 for shard in shards}
     for shard in shards:
-        take[shard] = -1 if take[shard] < half - 1 else take[shard]
+        take[shard] = -1 if take[shard] <= 2 else take[shard]
         assert take[shard] < first or take[shard] < uses(inside, shard)[0]
-    send = {k: 2 * (k - half) if k >= half else -1 for k in range(1, members)}
+    send = {k: k - 6 if k >= 6 else -1 for k in range(1, members)}
     give = []
     for cells in (outside, inside):
         steps, at = {}, 0
@@ -96,8 +93,8 @@
 
 
 def kernel(groups, members, pts_hbm, cnt_hbm, lat_hbm, prb_hbm, out, pts, cnt, lat, prb, xs, fi, fj, sums, parts, own, *rest):
-    us, ks = rest[:DEPTH], rest[DEPTH : 2 * DEPTH]
-    load, xsend, xrecv, psend, precv = rest[2 * DEPTH :]
+    us, vs, ks = rest[:DEPTH], rest[DEPTH : 2 * DEPTH], rest[2 * DEPTH : 3 * DEPTH]
+    load, xsend, xrecv, psend, precv = rest[3 * DEPTH :]
     row, col, layer = lax.axis_index("row"), lax.axis_index("col"), lax.axis_index("layer")
     a = row * 2 + lax.rem(col, 2)
     m = lax.div(col, 2) * 2 + layer
@@ -116,6 +113,11 @@
 
     def cols(j):
         return pl.ds(pl.multiple_of(j * SH, SH), SH)
+
+    barrier = pltpu.get_barrier_semaphore()
+    pl.semaphore_signal(barrier, inc=1, device_id=dev(b, m), device_id_type=MESH)
+    for k in range(1, members):
+        pl.semaphore_signal(barrier, inc=1, device_id=dev(a, mate(k)), device_id_type=MESH)
 
     pts[...] = jnp.zeros_like(pts)
     loads = [
@@ -124,11 +126,6 @@
     ]
     for copy in loads:
         copy.start()
-    barrier = pltpu.get_barrier_semaphore()
-    pl.semaphore_signal(barrier, inc=1, device_id=dev(b, m), device_id_type=MESH)
-    for k in range(1, members):
-        pl.semaphore_signal(barrier, inc=1, device_id=dev(a, mate(k)), device_id_type=MESH)
-
     sums[...] = jnp.zeros_like(sums)
     for k in ks:
         k[...] = jnp.zeros_like(k)
@@ -148,6 +145,13 @@
 
     def build_right(which, j):
         fj[which, :, cols(j)] = features(xs[which, j, 16:32, :])[1].astype(jnp.bfloat16)
+
+    def squares(si, rows, sj, at_cols):
+        left = fi[si, rows, :]
+        return [
+            jnp.dot(left, fj[sj, n * FEAT : (n + 1) * FEAT, at_cols], preferred_element_type=jnp.float32)
+            for n in range(2)
+        ]
 
     build_left(0, m)
     build_right(0, m)
@@ -155,7 +159,7 @@
         rows = pl.ds(pl.multiple_of(m * SH + first, BI), BI)
         for at in range(first, SH, BJ):
             at_cols = pl.ds(pl.multiple_of(m * SH + at, BJ), BJ)
-            k = entries(jnp.dot(fi[0, rows, :], fj[0, :, at_cols], preferred_element_type=jnp.float32))
+            k = entries(*squares(0, rows, 0, at_cols))
             term = jnp.dot(xs[0, m, 0:16, first : first + BI], k, preferred_element_type=jnp.float32)
             if first == 0:
                 own[:, at : at + BJ] = term
@@ -245,9 +249,10 @@
         at_cols = pl.ds(pl.multiple_of(j * SH + second, BJ), BJ)
         return si, rows, sj, at_cols, xs.at[si, i, 0:16, first : first + BI], xs.at[sj, j, 0:16, second : second + BJ]
 
-    def distance(at, n, u):
+    def distance(at, n):
         si, rows, sj, at_cols, _, _ = place(at, n)
-        u[...] = jnp.dot(fi[si, rows, :], fj[sj, :, at_cols], preferred_element_type=jnp.float32)
+        n = n % DEPTH
+        us[n][...], vs[n][...] = squares(si, rows, sj, at_cols)
 
     def products(at, n, k):
         si, rows, sj, at_cols, ci, cj = place(at, n)
@@ -318,7 +323,7 @@
 
     lax.fori_loop(0, lax.div(start, WIDE), early, 0)
     begin = cell(start)
-    distance(begin, 0, us[0])
+    distance(begin, 0)
 
     def step(p, carry):
         last, this, events, given = carry
@@ -334,15 +339,15 @@
         c = p * WIDE
         held = [this, *[cell(c + n) for n in range(1, WIDE + 1)]]
         for n in range(DEPTH):
-            distance(held[(n + 1) // TILES], n + 1, us[(n + 1) % DEPTH])
+            distance(held[(n + 1) // TILES], n + 1)
             products(held[(n - 1) // TILES] if n else last, n - 1, ks[(n - 1) % DEPTH])
-            ks[n][...] = entries(us[n][...])
+            ks[n][...] = entries(us[n][...], vs[n][...])
         return held[-2], held[-1], fetch_events(c + WIDE), give_events(c + WIDE)
 
     carry = (begin, begin, fetch_events(start), give_events(start))
     last, *_ = lax.fori_loop(lax.div(start, WIDE), steps // WIDE, step, carry)
     products(last, DEPTH - 1, ks[DEPTH - 1])
-    for n, kind, (which, k) in sorted(after_loop):
+    for n, kind, (which, k) in sorted(after_loop, key=lambda late: (-late[2][0], late[0])):
 
         @pl.when(inside if kind else jnp.logical_not(inside))
         def _(which=which, k=k):
@@ -379,11 +384,11 @@
             pltpu.VMEM((16, SH), jnp.float32),
             pltpu.VMEM((2, members, 32, SH), jnp.bfloat16),
             pltpu.VMEM((2, size, FEAT), jnp.bfloat16),
-            pltpu.VMEM((2, FEAT, size), jnp.bfloat16),
+            pltpu.VMEM((2, 2 * FEAT, size), jnp.bfloat16),
             pltpu.VMEM((2, 16, size), jnp.float32),
             pltpu.VMEM((2 * members, 16, SH), jnp.float32),
             pltpu.VMEM((16, SH), jnp.float32),
-            *[pltpu.VMEM((BI, BJ), jnp.float32)] * DEPTH,
+            *[pltpu.VMEM((BI, BJ), jnp.float32)] * (2 * DEPTH),
             *[pltpu.VMEM((BI, BJ), jnp.bfloat16)] * DEPTH,
             pltpu.SemaphoreType.DMA((4,)),
             pltpu.SemaphoreType.DMA((copies,)),

time: 123 us -> 112 us (0.911)
  Pallas kernels: 121 us -> 110 us
    pallas_call x1, Pallas kernels: 121 us -> 110 us  [local(): pl.pallas_call(functools.partial(kernel, groups, members), out_shape=jax....]
where the time goes in v4:
time: 112 us
  Pallas kernels  110 us (98%)
  local copies, waits for them, and re-layouts  1.47 us (1%)
    pallas_call x1, Pallas kernels, local(): pl.pallas_call(functools.partial(kernel, groups, members), out_shape=jax....  110 us

profile of v4, /device:TPU:1, one launch (start us, length us, event | category | flops | bytes accessed | tf_op | source)
XLA Modules:
  0.0 111.6 jit_solution(13686795196828567061)
XLA Ops:
  0.0 110.1 %shard_map.46 = f32[16,1024]{1,0:T(8,128)} custom-call(f32[3,1024]{1,0:T(4,128)} %pts_hbm.1, s32[1,1024]{1,0:T(1,128)} %bitcast.2, f32[1,1024]{1,0:T(1,128)} %bitcast.3, f32[16,1024]{1,0:T(8,128)} %prb_hbm.1), custom_call_target="tpu_custom_call" | custom-call | flops 10000000000 | bytes 10000000 | tf_op jit(solution)/shard_map/pallas_call | solution.py:375
  110.1 1.5 %copy.6 = f32[16,1024]{1,0:T(8,128)} copy(f32[16,1024]{1,0:T(8,128)} %shard_map.46) | data formatting | bytes 131072

commit v5 on v4

--- a/solution.py
+++ b/solution.py
@@ -18,7 +18,7 @@
 TILES = (SH // BI) * (SH // BJ)
 WIDE = 2
 DEPTH = TILES * WIDE
-FEAT = 48
+FEAT = 32
 
 L2E = math.log2(math.e)
 COORD = math.sqrt(5.0) / LENGTH * L2E
@@ -60,9 +60,13 @@
         high, mid, low = pieces(v)
         return jnp.where(at == 0, high, jnp.where(at == 1, mid, jnp.where(at == 2, low, 0.0)))
 
-    left = jnp.concatenate([hm, hm, hm, low, rows(norm), ones], axis=0)
-    right = [-2.0 * hm, -2.0 * mh, -2.0 * low, -2.0 * hm, ones]
-    return left, jnp.concatenate([*right, rows(norm), *right, rows(norm + C)], axis=0)
+    def other(v):
+        return jnp.roll(v, 4, axis=0)
+
+    hl = jnp.where(at < 3, hm, other(low))
+    left = jnp.concatenate([hm, hm, hl, rows(norm) + other(ones)], axis=0)
+    right = [-2.0 * hm, -2.0 * mh, -2.0 * other(hl)]
+    return left, jnp.concatenate([*right, ones + other(rows(norm)), *right, ones + other(rows(norm + C))], axis=0)
 
 
 def plan(members):

time: 112 us -> 110 us (0.982)
  Pallas kernels: 110 us -> 108 us
    pallas_call x1, Pallas kernels: 110 us -> 108 us  [local(): pl.pallas_call(functools.partial(kernel, groups, members), out_shape=jax....]
where the time goes in v5:
time: 110 us
  Pallas kernels  108 us (98%)
  local copies, waits for them, and re-layouts  1.47 us (1%)
    pallas_call x1, Pallas kernels, local(): pl.pallas_call(functools.partial(kernel, groups, members), out_shape=jax....  108 us

profile of v5, /device:TPU:1, one launch (start us, length us, event | category | flops | bytes accessed | tf_op | source)
XLA Modules:
  0.0 109.5 jit_solution(18219130853302448933)
XLA Ops:
  0.0 108.1 %shard_map.46 = f32[16,1024]{1,0:T(8,128)} custom-call(f32[3,1024]{1,0:T(4,128)} %pts_hbm.1, s32[1,1024]{1,0:T(1,128)} %bitcast.2, f32[1,1024]{1,0:T(1,128)} %bitcast.3, f32[16,1024]{1,0:T(8,128)} %prb_hbm.1), custom_call_target="tpu_custom_call" | custom-call | flops 10000000000 | bytes 10000000 | tf_op jit(solution)/shard_map/pallas_call | solution.py:379
  108.1 1.5 %copy.6 = f32[16,1024]{1,0:T(8,128)} copy(f32[16,1024]{1,0:T(8,128)} %shard_map.46) | data formatting | bytes 131072
